TPU v7x, 512 devices: a whole 4x8x8 slice. The times are simulated.
512 devices in a mesh: ens: 2 (over core), lat: 32 (over z, x), chan: 8 (over y).
Axes of the slice: x: 4, y: 8, z: 8, core: 2. Of those that a mesh axis runs over, the one named last changes fastest.
Arguments:
- field: bfloat16 [2, 384, 128, 256], P('ens', 'chan', 'lat'), may hold values from -6 to 6
- cotangent: bfloat16 [2, 384, 128, 256], P('ens', 'chan', 'lat'), may hold values from -6 to 6
- spec_weight: float32 [2, 64, 384], P(None, None, 'chan'), may hold values from -8 to 8
- disco_coef: float32 [128, 9], replicated, may hold values from -2 to 2
- disco_weight: float32 [9, 384], P(None, 'chan'), may hold values from -5 to 5
- disco_rows: int32 [128, 9], replicated, may hold values from 0 to 127, as said below
- disco_shift: int32 [128, 9], replicated, may hold values from -8 to 8
- w_hidden: bfloat16 [384, 768], replicated, may hold values from -0.3125 to 0.3125
- w_output: bfloat16 [768, 384], replicated, may hold values from -0.21875 to 0.21875
Outputs:
- grad_field: bfloat16 [2, 384, 128, 256], P('ens', 'chan', 'lat')
- grad_spec_weight: float32 [2, 64, 384], P(None, None, 'chan')
- grad_disco_weight: float32 [9, 384], P(None, 'chan')
- grad_w_hidden: float32 [384, 768], P('lat')
- grad_w_output: float32 [768, 384], P('lat')
Inputs may be any that keep to these rules, and one draw needn't show every extreme that they name: Entry k of row i of disco_rows names a latitude row within 2 rows of i.
All inputs are finite; a program needn't handle non-finite values.
Results may differ from a plain program's by a relative error of at most 0.013.
Values may be sent and summed in bfloat16 or wider, within the bound.
A program may use at most 64 MiB of HBM per device.

v0:
```python
import math
import jax
import jax.numpy as jnp
from jax import lax
from jax.sharding import PartitionSpec as P

HALO = 2
SHIFT = 8
norm_eps = 1e-06
inv_root_two = 0.7071067811865476
inv_root_tau = 0.3989422804014327
highest = lax.Precision.HIGHEST


def padded_2(block, sides, width):
    for axis, dim in sides:
        count = lax.axis_size(axis)
        forward = [(i, i + 1) for i in range(count - 1)]
        backward = [(target, source) for source, target in forward]
        low = lax.ppermute(
            lax.slice_in_dim(block, block.shape[dim] - width, None, axis=dim), axis, forward
        )
        high = lax.ppermute(lax.slice_in_dim(block, 0, width, axis=dim), axis, backward)
        block = jnp.concatenate([low, block, high], axis=dim)
    return block


def colatitudes(lat_count):
    return (jnp.arange(lat_count, dtype=jnp.int32).astype(jnp.float32) + 0.5) * (
        math.pi / lat_count
    )


def legendre_rows(first_order, order_count, lat_count, degree_count):
    colatitude = colatitudes(lat_count)
    cosine = jnp.cos(colatitude)
    sine_rows = jnp.sin(colatitude)
    orders = (first_order + jnp.arange(order_count, dtype=jnp.int32)).astype(jnp.float32)
    log_start = 0.5 * (
        jnp.log((2.0 * orders + 1.0) / (4.0 * math.pi))
        + lax.lgamma(orders + 0.5)
        - lax.lgamma(orders + 1.0)
        - 0.5 * math.log(math.pi)
    )
    diagonal = jnp.exp(log_start[:, None] + orders[:, None] * jnp.log(sine_rows)[None, :])

    def advance(carry, degree):
        previous, before = carry
        degree_value = degree.astype(jnp.float32)
        above = degree_value > orders
        upper_term = jnp.where(above, 4.0 * degree_value * degree_value - 1.0, 1.0)
        lower_term = jnp.where(above, degree_value * degree_value - orders * orders, 1.0)
        factor = jnp.sqrt(upper_term / lower_term)
        behind = jnp.where(
            above, (degree_value - 1.0) * (degree_value - 1.0) - orders * orders, 0.0
        )
        damping = jnp.sqrt(behind / (4.0 * (degree_value - 1.0) * (degree_value - 1.0) - 1.0))
        recurred = factor[:, None] * (cosine[None, :] * previous - damping[:, None] * before)
        current = jnp.where(
            above[:, None], recurred, jnp.where((degree_value == orders)[:, None], diagonal, 0.0)
        )
        return ((current, previous), current)

    zero_rows = jnp.zeros((order_count, lat_count), jnp.float32)
    finish, stacked = lax.scan(
        advance, (zero_rows, zero_rows), jnp.arange(degree_count, dtype=jnp.int32), unroll=True
    )
    return jnp.transpose(stacked, (1, 0, 2))


def quadrature(lat_count, lon_count):
    return 2.0 * math.pi / lon_count * (math.pi / lat_count) * jnp.sin(colatitudes(lat_count))


def lon_tables(lon_count, mode_count):
    columns = jnp.arange(lon_count, dtype=jnp.int32)
    mode_ids = jnp.arange(mode_count, dtype=jnp.int32)
    phase_ids = columns[:, None] * mode_ids[None, :] % lon_count
    angles = phase_ids.astype(jnp.float32) * (2.0 * math.pi / lon_count)
    cosine = jnp.cos(angles)
    sine_part = jnp.sin(angles)
    forward = jnp.concatenate([cosine, -sine_part], axis=1).astype(jnp.bfloat16)
    doubled = jnp.where(mode_ids == 0, 1.0, 2.0).astype(jnp.float32)[None, :]
    inverse = jnp.transpose(
        jnp.concatenate([doubled * cosine, -doubled * sine_part], axis=1)
    ).astype(jnp.bfloat16)
    return (forward, inverse)


def apply_filter(coeffs, spec_weight):
    real_weight = jnp.transpose(spec_weight[0])[:, None, :]
    imag_weight = jnp.transpose(spec_weight[1])[:, None, :]
    real_part = coeffs[:, 0]
    imag_part = coeffs[:, 1]
    return jnp.stack(
        [
            real_weight * real_part - imag_weight * imag_part,
            real_weight * imag_part + imag_weight * real_part,
        ],
        axis=1,
    )


def filter_adjoint(grads, coeffs, spec_weight):
    real_weight = jnp.transpose(spec_weight[0])[:, None, :]
    imag_weight = jnp.transpose(spec_weight[1])[:, None, :]
    grad_real = grads[:, 0]
    grad_imag = grads[:, 1]
    real_part = coeffs[:, 0]
    imag_part = coeffs[:, 1]
    weight_zero = jnp.transpose(jnp.sum(grad_real * real_part + grad_imag * imag_part, axis=1))
    weight_one = jnp.transpose(jnp.sum(grad_imag * real_part - grad_real * imag_part, axis=1))
    adjoint_coeffs = jnp.stack(
        [
            real_weight * grad_real + imag_weight * grad_imag,
            real_weight * grad_imag - imag_weight * grad_real,
        ],
        axis=1,
    )
    return (adjoint_coeffs, jnp.stack([weight_zero, weight_one], axis=0))


def mlp_backward(mixed_rows, adjoint_rows, w_hidden, w_output):
    mixed32 = mixed_rows.astype(jnp.float32)
    rscale = lax.rsqrt(jnp.mean(mixed32 * mixed32, axis=0, keepdims=True) + norm_eps)
    normed32 = mixed32 * rscale
    normed = normed32.astype(jnp.bfloat16)
    preact = lax.dot_general(
        w_hidden, normed, (((0,), (0,)), ((), ())), preferred_element_type=jnp.float32
    )
    activated = jax.nn.gelu(preact, approximate=False).astype(jnp.bfloat16)
    grad_output = lax.dot_general(
        activated, adjoint_rows, (((1,), (1,)), ((), ())), preferred_element_type=jnp.float32
    )
    grad_act = lax.dot_general(
        w_output, adjoint_rows, (((1,), (0,)), ((), ())), preferred_element_type=jnp.float32
    )
    cumulative = 0.5 * (1.0 + lax.erf(preact * inv_root_two))
    density = jnp.exp(-0.5 * preact * preact) * inv_root_tau
    grad_pre = (grad_act * (cumulative + preact * density)).astype(jnp.bfloat16)
    grad_hidden = lax.dot_general(
        normed, grad_pre, (((1,), (1,)), ((), ())), preferred_element_type=jnp.float32
    )
    grad_normed = lax.dot_general(
        w_hidden, grad_pre, (((1,), (0,)), ((), ())), preferred_element_type=jnp.float32
    )
    grad_mixed = (
        rscale * (grad_normed - normed32 * jnp.mean(grad_normed * normed32, axis=0, keepdims=True))
    ).astype(jnp.bfloat16)
    return (grad_mixed, grad_hidden, grad_output)


def to_modes(spectrum):
    return lax.all_to_all(spectrum, "lat", split_axis=3, concat_axis=1, tiled=True)


def to_bands(spectrum):
    return lax.all_to_all(spectrum, "lat", split_axis=1, concat_axis=3, tiled=True)


def wrap_lon(values, width):
    return jnp.concatenate([values[:, :, -width:], values, values[:, :, :width]], axis=2)


def disco_kernel(rows_tab, shift_tab, coef_tab, centre, disco_weight):
    row_step = rows_tab - centre[:, None] + HALO
    lon_step = shift_tab + SHIFT
    reach = jnp.arange(2 * HALO + 1, dtype=jnp.int32)
    span = jnp.arange(2 * SHIFT + 1, dtype=jnp.int32)
    onehot = (
        (row_step[:, :, None, None] == reach[None, None, :, None])
        & (lon_step[:, :, None, None] == span[None, None, None, :])
    ).astype(jnp.float32)
    kernel = jnp.einsum("rk,rkpq,kc->crpq", coef_tab, onehot, disco_weight, precision=highest)
    return (onehot, kernel)


def shards(
    field,
    cotangent,
    spec_weight,
    disco_coef,
    disco_weight,
    disco_rows,
    disco_shift,
    w_hidden,
    w_output,
):
    member = field[0]
    adjoint_member = cotangent[0]
    channels, lat_rows, lon_count = member.shape
    band_count = lax.axis_size("lat")
    lat_count = lat_rows * band_count
    mode_count = lat_count // 2
    modes_here = mode_count // band_count
    band_index = lax.axis_index("lat")
    first_row = band_index * lat_rows
    forward, inverse = lon_tables(lon_count, mode_count)
    legendre = legendre_rows(band_index * modes_here, modes_here, lat_count, mode_count)
    weighted = legendre * quadrature(lat_count, lon_count)[None, None, :]
    grad_scale = 1.0 / math.sqrt(lax.axis_size("ens") * lat_count * lon_count)
    reach_count = 2 * HALO + 1
    span_count = 2 * SHIFT + 1
    adjoint_rows = lax.all_to_all(adjoint_member, "chan", split_axis=2, concat_axis=0, tiled=True)
    spectrum = jnp.dot(
        member.reshape(channels * lat_rows, lon_count), forward, preferred_element_type=jnp.float32
    )
    spectrum = spectrum.astype(jnp.bfloat16).reshape(channels, lat_rows, 2, mode_count)
    mode_block = to_modes(spectrum)
    coeffs = jnp.einsum(
        "citm,mli->ctml", mode_block.astype(jnp.float32), weighted, precision=highest
    )
    synthesis = jnp.einsum(
        "ctml,mli->citm", apply_filter(coeffs, spec_weight), legendre, precision=highest
    ).astype(jnp.bfloat16)
    band_block = to_bands(synthesis)
    spectral = jnp.dot(
        band_block.reshape(channels * lat_rows, 2 * mode_count),
        inverse,
        preferred_element_type=jnp.float32,
    )
    spectral = spectral.reshape(channels, lat_rows, lon_count)
    global_rows = first_row + jnp.arange(lat_rows, dtype=jnp.int32)
    rows_here = lax.dynamic_slice_in_dim(disco_rows, first_row, lat_rows, 0)
    shift_here = lax.dynamic_slice_in_dim(disco_shift, first_row, lat_rows, 0)
    coef_here = lax.dynamic_slice_in_dim(disco_coef, first_row, lat_rows, 0)
    onehot_here, kernel_here = disco_kernel(
        rows_here, shift_here, coef_here, global_rows, disco_weight
    )
    padded = padded_2(member, (("lat", 1),), HALO)
    wide_field = wrap_lon(padded, SHIFT)
    disco_out = jnp.zeros((channels, lat_rows, lon_count), jnp.float32)
    for reach in range(reach_count):
        for span in range(span_count):
            window = wide_field[:, reach : reach + lat_rows, span : span + lon_count].astype(
                jnp.float32
            )
            disco_out = disco_out + kernel_here[:, :, reach, span][:, :, None] * window
    mixed_field = (spectral + disco_out).astype(jnp.bfloat16)
    mixed_rows = lax.all_to_all(mixed_field, "chan", split_axis=2, concat_axis=0, tiled=True)
    all_channels = mixed_rows.shape[0]
    row_width = mixed_rows.shape[2]
    grad_rows, grad_hidden, grad_output = mlp_backward(
        mixed_rows.reshape(all_channels, lat_rows * row_width),
        adjoint_rows.reshape(all_channels, lat_rows * row_width),
        w_hidden,
        w_output,
    )
    grad_field = lax.all_to_all(
        grad_rows.reshape(all_channels, lat_rows, row_width),
        "chan",
        split_axis=0,
        concat_axis=2,
        tiled=True,
    )
    grad_synth = lax.dot_general(
        grad_field.reshape(channels * lat_rows, lon_count),
        inverse,
        (((1,), (1,)), ((), ())),
        preferred_element_type=jnp.float32,
    )
    grad_synth = grad_synth.astype(jnp.bfloat16).reshape(channels, lat_rows, 2, mode_count)
    grad_modes = to_modes(grad_synth)
    grad_filtered = jnp.einsum(
        "citm,mli->ctml", grad_modes.astype(jnp.float32), legendre, precision=highest
    )
    grad_coeffs, filter_part = filter_adjoint(grad_filtered, coeffs, spec_weight)
    grad_spectrum = jnp.einsum("ctml,mli->citm", grad_coeffs, weighted, precision=highest).astype(
        jnp.bfloat16
    )
    grad_lines = to_bands(grad_spectrum)
    spectral_back = lax.dot_general(
        grad_lines.reshape(channels * lat_rows, 2 * mode_count),
        forward,
        (((1,), (1,)), ((), ())),
        preferred_element_type=jnp.float32,
    )
    spectral_back = spectral_back.reshape(channels, lat_rows, lon_count)
    grad_wide = grad_field.astype(jnp.float32)
    reach_sums = []
    for reach in range(reach_count):
        span_sums = []
        for span in range(span_count):
            window = wide_field[:, reach : reach + lat_rows, span : span + lon_count].astype(
                jnp.float32
            )
            span_sums.append(jnp.sum(window * grad_wide, axis=2))
        reach_sums.append(jnp.stack(span_sums, axis=2))
    inner_sum = jnp.stack(reach_sums, axis=2)
    disco_part = jnp.einsum(
        "ik,ikpq,cipq->kc", coef_here, onehot_here, inner_sum, precision=highest
    )
    rimmed = padded_2(grad_field, (("lat", 1),), HALO)
    wide_grads = wrap_lon(rimmed, SHIFT)
    ext_count = lat_rows + 2 * HALO
    ext_rows = first_row - HALO + jnp.arange(ext_count, dtype=jnp.int32)
    rows_ext = lax.dynamic_slice_in_dim(
        jnp.pad(disco_rows, ((HALO, HALO), (0, 0))), first_row, ext_count, 0
    )
    shift_ext = lax.dynamic_slice_in_dim(
        jnp.pad(disco_shift, ((HALO, HALO), (0, 0))), first_row, ext_count, 0
    )
    coef_ext = lax.dynamic_slice_in_dim(
        jnp.pad(disco_coef, ((HALO, HALO), (0, 0))), first_row, ext_count, 0
    )
    onehot_ext, kernel_ext = disco_kernel(rows_ext, shift_ext, coef_ext, ext_rows, disco_weight)
    spread = jnp.zeros((channels, lat_rows, lon_count), jnp.float32)
    for reach in range(reach_count):
        row_start = 2 * HALO - reach
        for span in range(span_count):
            col_start = 2 * SHIFT - span
            window = wide_grads[
                :, row_start : row_start + lat_rows, col_start : col_start + lon_count
            ].astype(jnp.float32)
            spread = (
                spread
                + kernel_ext[:, row_start : row_start + lat_rows, reach, span][:, :, None] * window
            )
    grad_input = (adjoint_member.astype(jnp.float32) + spectral_back + spread).astype(jnp.bfloat16)
    filter_total, disco_total = lax.psum((filter_part, disco_part), ("ens", "lat"))
    total_hidden, total_output = lax.psum((grad_hidden, grad_output), ("ens", "lat", "chan"))
    hidden_rows = total_hidden.shape[0] // band_count
    output_rows = total_output.shape[0] // band_count
    share_hidden = lax.dynamic_slice_in_dim(total_hidden, band_index * hidden_rows, hidden_rows, 0)
    share_output = lax.dynamic_slice_in_dim(total_output, band_index * output_rows, output_rows, 0)
    return (
        grad_input[None],
        filter_total,
        disco_total * grad_scale,
        share_hidden * grad_scale,
        share_output * grad_scale,
    )


def solution(mesh):
    in_specs = (
        P("ens", "chan", "lat", None),
        P("ens", "chan", "lat", None),
        P(None, None, "chan"),
        P(),
        P(None, "chan"),
        P(),
        P(),
        P(),
        P(),
    )
    out_specs = (
        P("ens", "chan", "lat", None),
        P(None, None, "chan"),
        P(None, "chan"),
        P("lat", None),
        P("lat", None),
    )
    return jax.shard_map(shards, mesh=mesh, in_specs=in_specs, out_specs=out_specs, check_vma=False)
```

profile of v0, /device:TPU:256, one launch (start us, length us, event | category | flops | bytes accessed | tf_op | source)
XLA Modules:
  0.0 485.7 jit_solution(5748793667730272015)
XLA Ops:
  7.2 0.3 negate_convert_fusion
  7.5 0.9 reshape_squeeze.3
  8.9 0.8 reshape.55196
  9.7 9.9 %all-to-all-start = ((bf16[32,2,384]{2,1,0:T(2,128)(2,1)}), bf16[32,2,384]{2,1,0:T(2,128)(2,1)S(1)}, u32[]{:S(2)}, u32[]{:S(2)}) async-start(bf16[32,2,384]{2,1,0:T(2,128)(2,1)} %reshape.55196), calls=%async_computation | async-start | bytes 98304 | tf_op jit(solution)/shard_map/all_to_all | solution.py:154
  19.6 3.4 collective-permute-start
  23.0 5.8 %collective-permute-start.1 = (bf16[48,2,256]{2,0,1:T(8,128)(2,1)S(1)}, bf16[48,2,256]{2,0,1:T(8,128)(2,1)S(1)}, u32[]{:S(2)}, u32[]{:S(2)}) collective-permute-start(bf16[48,2,256]{2,0,1:T(8,128)(2,1)S(1)} %get-tuple-element.536), channel_id=1, source_target_pairs={{8,0},{16,8},{24,16},{32,24},{40,32},{48,40},{56,48},{64,56},{72,6... | collective-permute-start | bytes 147464 | tf_op jit(solution)/shard_map/ppermute | solution.py:23
  28.8 0.7 fusion.693
  33.5 0.7 fusion.694
  45.7 0.7 fusion.695
  50.4 0.7 fusion.692
  73.4 0.6 convolution_bitcast_fusion.2
  74.1 0.6 fusion.684
  74.7 0.7 fusion.685
  75.4 0.7 fusion.686
  76.1 0.6 fusion.687
  77.1 0.9 convolution_bitcast_fusion
  78.1 0.6 fusion.680
  78.7 0.7 fusion.681
  80.2 0.3 multiply_convert_fusion.2
  83.6 0.4 broadcast_select_fusion
  84.4 0.3 select_select_fusion
  85.0 1.0 reshape.55202
  86.0 0.7 copy.394
  87.4 0.3 convolution_bitcast_fusion.5
  88.0 0.8 reshape.55198
  89.2 7.4 %all-to-all-start.1 = ((bf16[32,2,384]{2,1,0:T(2,128)(2,1)}), bf16[32,2,384]{2,1,0:T(2,128)(2,1)S(1)}, u32[]{:S(2)}, u32[]{:S(2)}) async-start(bf16[32,2,384]{2,1,0:T(2,128)(2,1)} %reshape.55198), calls=%async_computation.1 | async-start | bytes 98304 | tf_op jit(solution)/shard_map/all_to_all | solution.py:158
  96.8 4.9 %all-to-all-done.1 = bf16[32,2,384]{2,1,0:T(2,128)(2,1)S(1)} async-done(((bf16[32,2,384]{2,1,0:T(2,128)(2,1)}), bf16[32,2,384]{2,1,0:T(2,128)(2,1)S(1)}, u32[]{:S(2)}, u32[]{:S(2)}) %all-to-all-start.1) | async-done | bytes 49184 | tf_op jit(solution)/shard_map/all_to_all | solution.py:158
  101.7 7.1 %all-to-all-start.3 = ((bf16[8,2,3072]{2,1,0:T(2,128)(2,1)}), bf16[8,2,3072]{2,1,0:T(2,128)(2,1)S(1)}, u32[]{:S(2)}, u32[]{:S(2)}) async-start(bf16[8,2,3072]{2,1,0:T(2,128)(2,1)} %reshape.55202), calls=%async_computation.3 | async-start | bytes 196608 | tf_op jit(solution)/shard_map/all_to_all | solution.py:204
  109.5 6.0 %fusion.2 = bf16[48,4,256]{2,0,1:T(8,128)(2,1)S(1)} fusion(bf16[48,4,128]{0,2,1:T(8,128)(2,1)S(1)} %bitcast.623, bf16[48,4,256]{2,0,1:T(8,128)(2,1)S(1)} %bitcast.596, f32[48,4]{0,1:T(4,128)S(1)} %bitcast.820, f32[48,4]{0,1:T(4,128)S(1)} %bitcast.821, f32[48,4]{0,1:T(4,128)S(1)} %bitcast.822, f32[48,4]{0,1:T(4,128)S(1)} %bitcast.823, ...), kind=kOutput, calls=%fused_computation.173 | convolution fusion | flops 25493504 | bytes 8339200 | tf_op jit(solution)/shard_map/dot_general | solution.py:217
  115.7 1.0 reshape.55200
  116.7 0.8 all-to-all-done.3
  117.6 6.4 %all-to-all-start.2 = ((bf16[8,2,3072]{2,1,0:T(2,128)(2,1)}), bf16[8,2,3072]{2,1,0:T(2,128)(2,1)S(1)}, u32[]{:S(2)}, u32[]{:S(2)}) async-start(bf16[8,2,3072]{2,1,0:T(2,128)(2,1)} %reshape.55200), calls=%async_computation.2 | async-start | bytes 196608 | tf_op jit(solution)/shard_map/all_to_all | solution.py:240
  123.9 0.6 fusion.682
  125.2 7.5 %all-to-all-done.2 = bf16[8,2,3072]{2,1,0:T(2,128)(2,1)S(1)} async-done(((bf16[8,2,3072]{2,1,0:T(2,128)(2,1)}), bf16[8,2,3072]{2,1,0:T(2,128)(2,1)S(1)}, u32[]{:S(2)}, u32[]{:S(2)}) %all-to-all-start.2) | async-done | bytes 98336 | tf_op jit(solution)/shard_map/all_to_all | solution.py:240
  133.3 0.3 copy.376
  134.2 0.4 convolution_bitcast_fusion.1
  134.6 2.0 fusion.24
  136.7 0.3 fusion
  137.0 0.4 multiply_reduce_fusion
  137.8 1.0 reshape.55204
  138.8 3.4 all-to-all-start.4
  142.5 1.5 fusion.613
  144.0 6.9 %all-to-all-done.4 = bf16[8,2,3072]{2,1,0:T(2,128)(2,1)S(1)} async-done(((bf16[8,2,3072]{2,1,0:T(2,128)(2,1)}), bf16[8,2,3072]{2,1,0:T(2,128)(2,1)S(1)}, u32[]{:S(2)}, u32[]{:S(2)}) %all-to-all-start.4) | async-done | bytes 98336 | tf_op jit(solution)/shard_map/all_to_all | solution.py:249
  151.1 0.5 copy.433
  152.1 1.1 fusion.210
  153.2 1.2 fusion.219
  154.4 1.1 fusion.209
  155.5 1.2 fusion.218
  156.7 0.3 reshape.55185
  157.4 0.8 reshape.55206
  158.3 8.6 %all-to-all-start.5 = ((bf16[32,2,384]{2,1,0:T(2,128)(2,1)}), bf16[32,2,384]{2,1,0:T(2,128)(2,1)S(1)}, u32[]{:S(2)}, u32[]{:S(2)}) async-start(bf16[32,2,384]{2,1,0:T(2,128)(2,1)} %reshape.55206), calls=%async_computation.5 | async-start | bytes 98304 | tf_op jit(solution)/shard_map/all_to_all | solution.py:154
  166.9 3.4 collective-permute-start.2
  170.3 5.8 %collective-permute-start.3 = (bf16[48,2,256]{2,0,1:T(8,128)(2,1)S(1)}, bf16[48,2,256]{2,0,1:T(8,128)(2,1)S(1)}, u32[]{:S(2)}, u32[]{:S(2)}) collective-permute-start(bf16[48,2,256]{2,0,1:T(8,128)(2,1)S(1)} %get-tuple-element.534), channel_id=1, source_target_pairs={{8,0},{16,8},{24,16},{32,24},{40,32},{48,40},{56,48},{64,56},{72,6... | collective-permute-start | bytes 147464 | tf_op jit(solution)/shard_map/ppermute | solution.py:23
  176.1 0.8 fusion.217
  177.3 0.7 convolution_bitcast_fusion.6
  178.5 0.3 convolution_bitcast_fusion.4
  179.5 0.8 reshape.55208
  180.3 10.2 %all-to-all-start.6 = ((bf16[32,2,384]{2,1,0:T(2,128)(2,1)}), bf16[32,2,384]{2,1,0:T(2,128)(2,1)S(1)}, u32[]{:S(2)}, u32[]{:S(2)}) async-start(bf16[32,2,384]{2,1,0:T(2,128)(2,1)} %reshape.55208), calls=%async_computation.6 | async-start | bytes 98304 | tf_op jit(solution)/shard_map/all_to_all | solution.py:158
  190.5 276.9 %all-reduce.4 = (f32[2,64,48]{1,2,0:T(8,128)}, f32[9,48]{1,0:T(8,128)S(1)}) all-reduce(f32[2,64,48]{1,2,0:T(8,128)S(1)} %pad_maximum_fusion.8, f32[9,48]{1,0:T(8,128)S(1)} %convolution_bitcast_fusion.6), channel_id=1, replica_groups=mesh['ens'=2,'lat'=32,'chan'=8] {'ens','lat'}, use_global_device_ids=true, to_apply=%region_5.6 | all-reduce | flops 6576 | bytes 52608 | tf_op jit(solution)/shard_map/psum | solution.py:320
  467.5 0.6 broadcast_multiply_fusion
  468.7 6.5 %fusion.4 = bf16[1,48,4,256]{3,1,2,0:T(8,128)(2,1)S(1)} fusion(bf16[48,4,128]{0,2,1:T(8,128)(2,1)S(1)} %bitcast.622, bf16[48,4,256]{2,0,1:T(8,128)(2,1)S(1)} %all_to_all.100, bf16[48,8,256]{2,0,1:T(8,128)(2,1)S(1)} %get-tuple-element.539, bf16[48,8,8]{2,0,1:T(8,128)(2,1)S(1)} %get-tuple-element.520, bf16[48,8,8]{2,0,1:T(8,128)(2,1)S(1)} %get-tuple-element.519, ...), kind=kOutput, calls=%fused_computation.177 | convolution fusion | flops 37191680 | bytes 1076992 | tf_op jit(solution)/shard_map/dot_general | solution.py:272
  475.2 0.7 copy.395
  475.9 1.5 dynamic-slice_multiply_fusion
  477.5 1.4 dynamic-slice_multiply_fusion.1
  (409 shorter events, 12.2 us)
Async XLA Ops:
  7.2 127.0 %copy-start = (bf16[384,768]{1,0:T(8,128)(2,1)S(1)}, bf16[384,768]{1,0:T(8,128)(2,1)}, u32[]{:S(2)}) copy-start(bf16[384,768]{1,0:T(8,128)(2,1)} %param.16) | copy-start | bytes 1769476
  8.4 64.4 %copy-start.5 = (s32[128,9]{0,1:T(8,128)S(1)}, s32[128,9]{0,1:T(8,128)}, u32[]{:S(2)}) copy-start(s32[128,9]{0,1:T(8,128)} %param.15) | copy-start | bytes 13828
  8.6 64.4 %copy-start.6 = (s32[128,9]{0,1:T(8,128)S(1)}, s32[128,9]{0,1:T(8,128)}, u32[]{:S(2)}) copy-start(s32[128,9]{0,1:T(8,128)} %param.14) | copy-start | bytes 13828
  8.6 64.7 %copy-start.3 = (f32[128,9]{0,1:T(8,128)S(1)}, f32[128,9]{0,1:T(8,128)}, u32[]{:S(2)}) copy-start(f32[128,9]{0,1:T(8,128)} %param.12) | copy-start | bytes 13828
  8.6 64.8 %copy-start.82 = (f32[9,48]{1,0:T(8,128)S(1)}, f32[9,48]{1,0:T(8,128)}, u32[]{:S(2)}) copy-start(f32[9,48]{1,0:T(8,128)} %param.13) | copy-start | bytes 5188
  9.7 77.4 %all-to-all-start = ((bf16[32,2,384]{2,1,0:T(2,128)(2,1)}), bf16[32,2,384]{2,1,0:T(2,128)(2,1)S(1)}, u32[]{:S(2)}, u32[]{:S(2)}) async-start(bf16[32,2,384]{2,1,0:T(2,128)(2,1)} %reshape.55196), calls=%async_computation | async-start | bytes 98304 | tf_op jit(solution)/shard_map/all_to_all | solution.py:154
  19.6 67.3 %collective-permute-start = (bf16[48,2,256]{2,0,1:T(8,128)(2,1)S(1)}, bf16[48,2,256]{2,0,1:T(8,128)(2,1)S(1)}, u32[]{:S(2)}, u32[]{:S(2)}) collective-permute-start(bf16[48,2,256]{2,0,1:T(8,128)(2,1)S(1)} %get-tuple-element.537), channel_id=1, source_target_pairs={{0,8},{8,16},{16,24},{24,32},{32,40},{40,48},{48,56},{56,64},{64,7... | collective-permute-start | bytes 147464 | tf_op jit(solution)/shard_map/ppermute | solution.py:20
  23.0 63.9 %collective-permute-start.1 = (bf16[48,2,256]{2,0,1:T(8,128)(2,1)S(1)}, bf16[48,2,256]{2,0,1:T(8,128)(2,1)S(1)}, u32[]{:S(2)}, u32[]{:S(2)}) collective-permute-start(bf16[48,2,256]{2,0,1:T(8,128)(2,1)S(1)} %get-tuple-element.536), channel_id=1, source_target_pairs={{8,0},{16,8},{24,16},{32,24},{40,32},{48,40},{56,48},{64,56},{72,6... | collective-permute-start | bytes 147464 | tf_op jit(solution)/shard_map/ppermute | solution.py:23
  88.9 20.3 %copy-start.36 = (f32[48,4,1,1]{0,3,2,1:T(1,128)S(1)}, f32[48,4,1,1]{0,3,2,1:T(1,128)}, u32[]{:S(2)}) copy-start(f32[48,4,1,1]{0,3,2,1:T(1,128)} %get-tuple-element.462) | copy-start | bytes 2308
  88.9 20.3 %copy-start.37 = (f32[48,4,1,1]{0,3,2,1:T(1,128)S(1)}, f32[48,4,1,1]{0,3,2,1:T(1,128)}, u32[]{:S(2)}) copy-start(f32[48,4,1,1]{0,3,2,1:T(1,128)} %get-tuple-element.463) | copy-start | bytes 2308
  88.9 20.3 %copy-start.38 = (f32[48,4,1,1]{0,3,2,1:T(1,128)S(1)}, f32[48,4,1,1]{0,3,2,1:T(1,128)}, u32[]{:S(2)}) copy-start(f32[48,4,1,1]{0,3,2,1:T(1,128)} %get-tuple-element.464) | copy-start | bytes 2308
  88.9 20.3 %copy-start.39 = (f32[48,4,1,1]{0,3,2,1:T(1,128)S(1)}, f32[48,4,1,1]{0,3,2,1:T(1,128)}, u32[]{:S(2)}) copy-start(f32[48,4,1,1]{0,3,2,1:T(1,128)} %get-tuple-element.465) | copy-start | bytes 2308
  88.9 20.3 %copy-start.40 = (f32[48,4,1,1]{0,3,2,1:T(1,128)S(1)}, f32[48,4,1,1]{0,3,2,1:T(1,128)}, u32[]{:S(2)}) copy-start(f32[48,4,1,1]{0,3,2,1:T(1,128)} %get-tuple-element.466) | copy-start | bytes 2308
  88.9 20.3 %copy-start.41 = (f32[48,4,1,1]{0,3,2,1:T(1,128)S(1)}, f32[48,4,1,1]{0,3,2,1:T(1,128)}, u32[]{:S(2)}) copy-start(f32[48,4,1,1]{0,3,2,1:T(1,128)} %get-tuple-element.467) | copy-start | bytes 2308
  88.9 20.3 %copy-start.42 = (f32[48,4,1,1]{0,3,2,1:T(1,128)S(1)}, f32[48,4,1,1]{0,3,2,1:T(1,128)}, u32[]{:S(2)}) copy-start(f32[48,4,1,1]{0,3,2,1:T(1,128)} %get-tuple-element.468) | copy-start | bytes 2308
  88.9 20.3 %copy-start.43 = (f32[48,4,1,1]{0,3,2,1:T(1,128)S(1)}, f32[48,4,1,1]{0,3,2,1:T(1,128)}, u32[]{:S(2)}) copy-start(f32[48,4,1,1]{0,3,2,1:T(1,128)} %get-tuple-element.469) | copy-start | bytes 2308
  88.9 20.3 %copy-start.44 = (f32[48,4,1,1]{0,3,2,1:T(1,128)S(1)}, f32[48,4,1,1]{0,3,2,1:T(1,128)}, u32[]{:S(2)}) copy-start(f32[48,4,1,1]{0,3,2,1:T(1,128)} %get-tuple-element.470) | copy-start | bytes 2308
  89.0 20.3 %copy-start.45 = (f32[48,4,1,1]{0,3,2,1:T(1,128)S(1)}, f32[48,4,1,1]{0,3,2,1:T(1,128)}, u32[]{:S(2)}) copy-start(f32[48,4,1,1]{0,3,2,1:T(1,128)} %get-tuple-element.471) | copy-start | bytes 2308
  89.0 20.3 %copy-start.46 = (f32[48,4,1,1]{0,3,2,1:T(1,128)S(1)}, f32[48,4,1,1]{0,3,2,1:T(1,128)}, u32[]{:S(2)}) copy-start(f32[48,4,1,1]{0,3,2,1:T(1,128)} %get-tuple-element.472) | copy-start | bytes 2308
  89.0 20.3 %copy-start.47 = (f32[48,4,1,1]{0,3,2,1:T(1,128)S(1)}, f32[48,4,1,1]{0,3,2,1:T(1,128)}, u32[]{:S(2)}) copy-start(f32[48,4,1,1]{0,3,2,1:T(1,128)} %get-tuple-element.473) | copy-start | bytes 2308
  89.0 20.3 %copy-start.48 = (f32[48,4,1,1]{0,3,2,1:T(1,128)S(1)}, f32[48,4,1,1]{0,3,2,1:T(1,128)}, u32[]{:S(2)}) copy-start(f32[48,4,1,1]{0,3,2,1:T(1,128)} %get-tuple-element.474) | copy-start | bytes 2308
  89.2 12.5 %all-to-all-start.1 = ((bf16[32,2,384]{2,1,0:T(2,128)(2,1)}), bf16[32,2,384]{2,1,0:T(2,128)(2,1)S(1)}, u32[]{:S(2)}, u32[]{:S(2)}) async-start(bf16[32,2,384]{2,1,0:T(2,128)(2,1)} %reshape.55198), calls=%async_computation.1 | async-start | bytes 98304 | tf_op jit(solution)/shard_map/all_to_all | solution.py:158
  101.7 15.8 %all-to-all-start.3 = ((bf16[8,2,3072]{2,1,0:T(2,128)(2,1)}), bf16[8,2,3072]{2,1,0:T(2,128)(2,1)S(1)}, u32[]{:S(2)}, u32[]{:S(2)}) async-start(bf16[8,2,3072]{2,1,0:T(2,128)(2,1)} %reshape.55202), calls=%async_computation.3 | async-start | bytes 196608 | tf_op jit(solution)/shard_map/all_to_all | solution.py:204
  117.6 15.1 %all-to-all-start.2 = ((bf16[8,2,3072]{2,1,0:T(2,128)(2,1)}), bf16[8,2,3072]{2,1,0:T(2,128)(2,1)S(1)}, u32[]{:S(2)}, u32[]{:S(2)}) async-start(bf16[8,2,3072]{2,1,0:T(2,128)(2,1)} %reshape.55200), calls=%async_computation.2 | async-start | bytes 196608 | tf_op jit(solution)/shard_map/all_to_all | solution.py:240
  138.8 12.0 %all-to-all-start.4 = ((bf16[8,2,3072]{2,1,0:T(2,128)(2,1)}), bf16[8,2,3072]{2,1,0:T(2,128)(2,1)S(1)}, u32[]{:S(2)}, u32[]{:S(2)}) async-start(bf16[8,2,3072]{2,1,0:T(2,128)(2,1)} %reshape.55204), calls=%async_computation.4 | async-start | bytes 196608 | tf_op jit(solution)/shard_map/all_to_all | solution.py:249
  142.2 333.7 %all-reduce.7.cloned.1.call-start = ((), (), s32[]{:S(2)}) async-start(), calls=%async_computation.7 | async-start | bytes 4718592 | tf_op jit(solution)/shard_map/psum | solution.py:321
  158.3 19.9 %all-to-all-start.5 = ((bf16[32,2,384]{2,1,0:T(2,128)(2,1)}), bf16[32,2,384]{2,1,0:T(2,128)(2,1)S(1)}, u32[]{:S(2)}, u32[]{:S(2)}) async-start(bf16[32,2,384]{2,1,0:T(2,128)(2,1)} %reshape.55206), calls=%async_computation.5 | async-start | bytes 98304 | tf_op jit(solution)/shard_map/all_to_all | solution.py:154
  166.9 11.1 %collective-permute-start.2 = (bf16[48,2,256]{2,0,1:T(8,128)(2,1)S(1)}, bf16[48,2,256]{2,0,1:T(8,128)(2,1)S(1)}, u32[]{:S(2)}, u32[]{:S(2)}) collective-permute-start(bf16[48,2,256]{2,0,1:T(8,128)(2,1)S(1)} %get-tuple-element.535), channel_id=1, source_target_pairs={{0,8},{8,16},{16,24},{24,32},{32,40},{40,48},{48,56},{56,64},{64,7... | collective-permute-start | bytes 147464 | tf_op jit(solution)/shard_map/ppermute | solution.py:20
  170.3 7.8 %collective-permute-start.3 = (bf16[48,2,256]{2,0,1:T(8,128)(2,1)S(1)}, bf16[48,2,256]{2,0,1:T(8,128)(2,1)S(1)}, u32[]{:S(2)}, u32[]{:S(2)}) collective-permute-start(bf16[48,2,256]{2,0,1:T(8,128)(2,1)S(1)} %get-tuple-element.534), channel_id=1, source_target_pairs={{8,0},{16,8},{24,16},{32,24},{40,32},{48,40},{56,48},{64,56},{72,6... | collective-permute-start | bytes 147464 | tf_op jit(solution)/shard_map/ppermute | solution.py:23
  178.8 289.6 %copy-start.7 = (f32[48,4,1,1]{0,3,2,1:T(1,128)S(1)}, f32[48,4,1,1]{0,3,2,1:T(1,128)}, u32[]{:S(2)}) copy-start(f32[48,4,1,1]{0,3,2,1:T(1,128)} %get-tuple-element.400) | copy-start | bytes 2308
  178.8 289.6 %copy-start.8 = (f32[48,4,1,1]{0,3,2,1:T(1,128)S(1)}, f32[48,4,1,1]{0,3,2,1:T(1,128)}, u32[]{:S(2)}) copy-start(f32[48,4,1,1]{0,3,2,1:T(1,128)} %get-tuple-element.401) | copy-start | bytes 2308
  178.8 289.6 %copy-start.9 = (f32[48,4,1,1]{0,3,2,1:T(1,128)S(1)}, f32[48,4,1,1]{0,3,2,1:T(1,128)}, u32[]{:S(2)}) copy-start(f32[48,4,1,1]{0,3,2,1:T(1,128)} %get-tuple-element.402) | copy-start | bytes 2308
  178.8 289.6 %copy-start.10 = (f32[48,4,1,1]{0,3,2,1:T(1,128)S(1)}, f32[48,4,1,1]{0,3,2,1:T(1,128)}, u32[]{:S(2)}) copy-start(f32[48,4,1,1]{0,3,2,1:T(1,128)} %get-tuple-element.403) | copy-start | bytes 2308
  178.8 289.6 %copy-start.11 = (f32[48,4,1,1]{0,3,2,1:T(1,128)S(1)}, f32[48,4,1,1]{0,3,2,1:T(1,128)}, u32[]{:S(2)}) copy-start(f32[48,4,1,1]{0,3,2,1:T(1,128)} %get-tuple-element.404) | copy-start | bytes 2308
  178.8 289.6 %copy-start.12 = (f32[48,4,1,1]{0,3,2,1:T(1,128)S(1)}, f32[48,4,1,1]{0,3,2,1:T(1,128)}, u32[]{:S(2)}) copy-start(f32[48,4,1,1]{0,3,2,1:T(1,128)} %get-tuple-element.405) | copy-start | bytes 2308
  178.8 289.6 %copy-start.13 = (f32[48,4,1,1]{0,3,2,1:T(1,128)S(1)}, f32[48,4,1,1]{0,3,2,1:T(1,128)}, u32[]{:S(2)}) copy-start(f32[48,4,1,1]{0,3,2,1:T(1,128)} %get-tuple-element.406) | copy-start | bytes 2308
  178.8 289.6 %copy-start.14 = (f32[48,4,1,1]{0,3,2,1:T(1,128)S(1)}, f32[48,4,1,1]{0,3,2,1:T(1,128)}, u32[]{:S(2)}) copy-start(f32[48,4,1,1]{0,3,2,1:T(1,128)} %get-tuple-element.407) | copy-start | bytes 2308
  178.9 289.6 %copy-start.15 = (f32[48,4,1,1]{0,3,2,1:T(1,128)S(1)}, f32[48,4,1,1]{0,3,2,1:T(1,128)}, u32[]{:S(2)}) copy-start(f32[48,4,1,1]{0,3,2,1:T(1,128)} %get-tuple-element.408) | copy-start | bytes 2308
  178.9 289.6 %copy-start.16 = (f32[48,4,1,1]{0,3,2,1:T(1,128)S(1)}, f32[48,4,1,1]{0,3,2,1:T(1,128)}, u32[]{:S(2)}) copy-start(f32[48,4,1,1]{0,3,2,1:T(1,128)} %get-tuple-element.409) | copy-start | bytes 2308
  178.9 289.6 %copy-start.17 = (f32[48,4,1,1]{0,3,2,1:T(1,128)S(1)}, f32[48,4,1,1]{0,3,2,1:T(1,128)}, u32[]{:S(2)}) copy-start(f32[48,4,1,1]{0,3,2,1:T(1,128)} %get-tuple-element.410) | copy-start | bytes 2308
  178.9 289.6 %copy-start.18 = (f32[48,4,1,1]{0,3,2,1:T(1,128)S(1)}, f32[48,4,1,1]{0,3,2,1:T(1,128)}, u32[]{:S(2)}) copy-start(f32[48,4,1,1]{0,3,2,1:T(1,128)} %get-tuple-element.411) | copy-start | bytes 2308
  178.9 289.6 %copy-start.19 = (f32[48,4,1,1]{0,3,2,1:T(1,128)S(1)}, f32[48,4,1,1]{0,3,2,1:T(1,128)}, u32[]{:S(2)}) copy-start(f32[48,4,1,1]{0,3,2,1:T(1,128)} %get-tuple-element.412) | copy-start | bytes 2308
  178.9 289.6 %copy-start.20 = (f32[48,4,1,1]{0,3,2,1:T(1,128)S(1)}, f32[48,4,1,1]{0,3,2,1:T(1,128)}, u32[]{:S(2)}) copy-start(f32[48,4,1,1]{0,3,2,1:T(1,128)} %get-tuple-element.413) | copy-start | bytes 2308
  178.9 289.6 %copy-start.21 = (f32[48,4,1,1]{0,3,2,1:T(1,128)S(1)}, f32[48,4,1,1]{0,3,2,1:T(1,128)}, u32[]{:S(2)}) copy-start(f32[48,4,1,1]{0,3,2,1:T(1,128)} %get-tuple-element.414) | copy-start | bytes 2308
  178.9 289.6 %copy-start.22 = (f32[48,4,1,1]{0,3,2,1:T(1,128)S(1)}, f32[48,4,1,1]{0,3,2,1:T(1,128)}, u32[]{:S(2)}) copy-start(f32[48,4,1,1]{0,3,2,1:T(1,128)} %get-tuple-element.415) | copy-start | bytes 2308
  178.9 289.6 %copy-start.23 = (f32[48,4,1,1]{0,3,2,1:T(1,128)S(1)}, f32[48,4,1,1]{0,3,2,1:T(1,128)}, u32[]{:S(2)}) copy-start(f32[48,4,1,1]{0,3,2,1:T(1,128)} %get-tuple-element.416) | copy-start | bytes 2308
  178.9 289.6 %copy-start.24 = (f32[48,4,1,1]{0,3,2,1:T(1,128)S(1)}, f32[48,4,1,1]{0,3,2,1:T(1,128)}, u32[]{:S(2)}) copy-start(f32[48,4,1,1]{0,3,2,1:T(1,128)} %get-tuple-element.417) | copy-start | bytes 2308
  179.0 289.6 %copy-start.25 = (f32[48,4,1,1]{0,3,2,1:T(1,128)S(1)}, f32[48,4,1,1]{0,3,2,1:T(1,128)}, u32[]{:S(2)}) copy-start(f32[48,4,1,1]{0,3,2,1:T(1,128)} %get-tuple-element.418) | copy-start | bytes 2308
  179.0 289.6 %copy-start.26 = (f32[48,4,1,1]{0,3,2,1:T(1,128)S(1)}, f32[48,4,1,1]{0,3,2,1:T(1,128)}, u32[]{:S(2)}) copy-start(f32[48,4,1,1]{0,3,2,1:T(1,128)} %get-tuple-element.419) | copy-start | bytes 2308
  179.0 289.6 %copy-start.27 = (f32[48,4,1,1]{0,3,2,1:T(1,128)S(1)}, f32[48,4,1,1]{0,3,2,1:T(1,128)}, u32[]{:S(2)}) copy-start(f32[48,4,1,1]{0,3,2,1:T(1,128)} %get-tuple-element.420) | copy-start | bytes 2308
  179.0 289.6 %copy-start.28 = (f32[48,4,1,1]{0,3,2,1:T(1,128)S(1)}, f32[48,4,1,1]{0,3,2,1:T(1,128)}, u32[]{:S(2)}) copy-start(f32[48,4,1,1]{0,3,2,1:T(1,128)} %get-tuple-element.421) | copy-start | bytes 2308
  179.0 289.6 %copy-start.29 = (f32[48,4,1,1]{0,3,2,1:T(1,128)S(1)}, f32[48,4,1,1]{0,3,2,1:T(1,128)}, u32[]{:S(2)}) copy-start(f32[48,4,1,1]{0,3,2,1:T(1,128)} %get-tuple-element.422) | copy-start | bytes 2308
  179.0 289.6 %copy-start.30 = (f32[48,4,1,1]{0,3,2,1:T(1,128)S(1)}, f32[48,4,1,1]{0,3,2,1:T(1,128)}, u32[]{:S(2)}) copy-start(f32[48,4,1,1]{0,3,2,1:T(1,128)} %get-tuple-element.423) | copy-start | bytes 2308
  179.0 289.6 %copy-start.31 = (f32[48,4,1,1]{0,3,2,1:T(1,128)S(1)}, f32[48,4,1,1]{0,3,2,1:T(1,128)}, u32[]{:S(2)}) copy-start(f32[48,4,1,1]{0,3,2,1:T(1,128)} %get-tuple-element.424) | copy-start | bytes 2308
  179.0 289.6 %copy-start.72 = (f32[48,4,1,1]{0,3,2,1:T(1,128)S(1)}, f32[48,4,1,1]{0,3,2,1:T(1,128)}, u32[]{:S(2)}) copy-start(f32[48,4,1,1]{0,3,2,1:T(1,128)} %get-tuple-element.425) | copy-start | bytes 2308
  179.0 289.6 %copy-start.73 = (f32[48,4,1,1]{0,3,2,1:T(1,128)S(1)}, f32[48,4,1,1]{0,3,2,1:T(1,128)}, u32[]{:S(2)}) copy-start(f32[48,4,1,1]{0,3,2,1:T(1,128)} %get-tuple-element.426) | copy-start | bytes 2308
  179.0 289.6 %copy-start.74 = (f32[48,4,1,1]{0,3,2,1:T(1,128)S(1)}, f32[48,4,1,1]{0,3,2,1:T(1,128)}, u32[]{:S(2)}) copy-start(f32[48,4,1,1]{0,3,2,1:T(1,128)} %get-tuple-element.427) | copy-start | bytes 2308
  179.1 289.6 %copy-start.75 = (f32[48,4,1,1]{0,3,2,1:T(1,128)S(1)}, f32[48,4,1,1]{0,3,2,1:T(1,128)}, u32[]{:S(2)}) copy-start(f32[48,4,1,1]{0,3,2,1:T(1,128)} %get-tuple-element.428) | copy-start | bytes 2308
  179.1 289.6 %copy-start.76 = (f32[48,4,1,1]{0,3,2,1:T(1,128)S(1)}, f32[48,4,1,1]{0,3,2,1:T(1,128)}, u32[]{:S(2)}) copy-start(f32[48,4,1,1]{0,3,2,1:T(1,128)} %get-tuple-element.429) | copy-start | bytes 2308
  179.1 289.6 %copy-start.77 = (f32[48,4,1,1]{0,3,2,1:T(1,128)S(1)}, f32[48,4,1,1]{0,3,2,1:T(1,128)}, u32[]{:S(2)}) copy-start(f32[48,4,1,1]{0,3,2,1:T(1,128)} %get-tuple-element.430) | copy-start | bytes 2308
  179.1 289.6 %copy-start.78 = (f32[48,4,1,1]{0,3,2,1:T(1,128)S(1)}, f32[48,4,1,1]{0,3,2,1:T(1,128)}, u32[]{:S(2)}) copy-start(f32[48,4,1,1]{0,3,2,1:T(1,128)} %get-tuple-element.431) | copy-start | bytes 2308
  179.1 289.6 %copy-start.79 = (f32[48,4,1,1]{0,3,2,1:T(1,128)S(1)}, f32[48,4,1,1]{0,3,2,1:T(1,128)}, u32[]{:S(2)}) copy-start(f32[48,4,1,1]{0,3,2,1:T(1,128)} %get-tuple-element.432) | copy-start | bytes 2308
  179.1 289.6 %copy-start.80 = (f32[48,4,1,1]{0,3,2,1:T(1,128)S(1)}, f32[48,4,1,1]{0,3,2,1:T(1,128)}, u32[]{:S(2)}) copy-start(f32[48,4,1,1]{0,3,2,1:T(1,128)} %get-tuple-element.433) | copy-start | bytes 2308
  180.3 287.7 %all-to-all-start.6 = ((bf16[32,2,384]{2,1,0:T(2,128)(2,1)}), bf16[32,2,384]{2,1,0:T(2,128)(2,1)S(1)}, u32[]{:S(2)}, u32[]{:S(2)}) async-start(bf16[32,2,384]{2,1,0:T(2,128)(2,1)} %reshape.55208), calls=%async_computation.6 | async-start | bytes 98304 | tf_op jit(solution)/shard_map/all_to_all | solution.py:158
  (31 other events, 563.7 us)
Sparse Core Ops, SparseCore 0:
  148.1 279.6 all-reduce.6
where the time goes:
time: 487 us; the launch traced here: 486 us
  blocking collectives  277 us (57%)
  starting transfers between devices  71.5 us (15%)
  between operations  58.2 us (12%)
  local copies, waits for them, and re-layouts  24.1 us (5%)
  matrix products  20.6 us (4%)
  waiting for transfers between devices  20.2 us (4%)
  other arithmetic  14.3 us (3%)
    psum x1, blocking collectives, shards(): lax.psum((filter_part, disco_part), ('ens', 'lat'))  277 us
    all_to_all x2, starting transfers between devices, to_modes(): lax.all_to_all(spectrum, 'lat', split_axis=3, concat_axis=1, tiled=True)  18.5 us
    all_to_all x2, starting transfers between devices, to_bands(): lax.all_to_all(spectrum, 'lat', split_axis=1, concat_axis=3, tiled=True)  17.6 us
    ppermute x2, starting transfers between devices, padded_2(): lax.ppermute(lax.slice_in_dim(block, 0, width, axis=dim), axis, backward)  11.6 us
  transfers between devices with their start and end apart: 12, of which 4 were waited for; matrix products, arithmetic and copies ran while one was open for 9% of the time, Pallas kernels for 0%

commit v1 on v0

--- a/solution.py
+++ b/solution.py
@@ -317,7 +317,7 @@
                 + kernel_ext[:, row_start : row_start + lat_rows, reach, span][:, :, None] * window
             )
     grad_input = (adjoint_member.astype(jnp.float32) + spectral_back + spread).astype(jnp.bfloat16)
-    filter_total, disco_total = lax.psum((filter_part, disco_part), ("ens", "lat"))
+    filter_total, disco_total = lax.psum(lax.psum((filter_part, disco_part), "ens"), "lat")
     total_hidden, total_output = lax.psum((grad_hidden, grad_output), ("ens", "lat", "chan"))
     hidden_rows = total_hidden.shape[0] // band_count
     output_rows = total_output.shape[0] // band_count

time: 487 us -> 444 us (0.912)
  the two profiles are of different devices: /device:TPU:256 before, /device:TPU:1 now
where the time goes in v1:
time: 444 us; the launch traced here: 443 us
  waiting for transfers between devices  133 us (30%)
  blocking collectives  127 us (29%)
  starting transfers between devices  65.2 us (15%)
  between operations  58 us (13%)
  local copies, waits for them, and re-layouts  24.1 us (5%)
  matrix products  20.6 us (5%)
  other arithmetic  14.3 us (3%)
    psum x1, blocking collectives, shards(): lax.psum(lax.psum((filter_part, disco_part), 'ens'), 'lat')  116 us
    psum x1, waiting for transfers between devices, shards(): lax.psum((grad_hidden, grad_output), ('ens', 'lat', 'chan'))  110 us
    all_to_all x2, starting transfers between devices, to_bands(): lax.all_to_all(spectrum, 'lat', split_axis=1, concat_axis=3, tiled=True)  21.8 us
    all_to_all x2, starting transfers between devices, to_modes(): lax.all_to_all(spectrum, 'lat', split_axis=3, concat_axis=1, tiled=True)  17.6 us
    psum x1, blocking collectives, shards(): lax.psum((filter_part, disco_part), 'ens')  11.8 us
    unnamed x193, local copies, waits for them, and re-layouts  9.26 us
  transfers between devices with their start and end apart: 12, of which 6 were waited for; matrix products, arithmetic and copies ran while one was open for 10% of the time, Pallas kernels for 0%

profile of v1, /device:TPU:1, one launch (start us, length us, event | category | flops | bytes accessed | tf_op | source)
XLA Modules:
  0.0 442.6 jit_solution(13903442897942134869)
XLA Ops:
  7.2 0.3 negate_convert_fusion
  7.5 0.9 reshape_squeeze.3
  8.9 0.8 reshape.55196
  9.7 13.7 %all-to-all-start = ((bf16[32,2,384]{2,1,0:T(2,128)(2,1)}), bf16[32,2,384]{2,1,0:T(2,128)(2,1)S(1)}, u32[]{:S(2)}, u32[]{:S(2)}) async-start(bf16[32,2,384]{2,1,0:T(2,128)(2,1)} %reshape.55196), calls=%async_computation | async-start | bytes 98304 | tf_op jit(solution)/shard_map/all_to_all | solution.py:154
  23.5 3.1 collective-permute-start
  26.6 1.3 collective-permute-start.1
  27.9 0.7 fusion.693
  32.5 0.7 fusion.694
  44.8 0.7 fusion.695
  49.3 0.7 fusion.692
  72.4 0.6 convolution_bitcast_fusion.2
  73.1 0.7 fusion.684
  73.7 0.7 fusion.685
  74.4 0.7 fusion.686
  75.1 0.6 fusion.687
  76.0 0.9 convolution_bitcast_fusion
  77.0 0.6 fusion.680
  77.7 0.7 fusion.681
  82.6 0.4 broadcast_select_fusion
  83.4 0.3 select_select_fusion
  84.0 1.0 reshape.55202
  85.0 0.7 copy.394
  86.3 0.3 convolution_bitcast_fusion.5
  87.0 0.8 reshape.55198
  88.2 11.0 %all-to-all-start.1 = ((bf16[32,2,384]{2,1,0:T(2,128)(2,1)}), bf16[32,2,384]{2,1,0:T(2,128)(2,1)S(1)}, u32[]{:S(2)}, u32[]{:S(2)}) async-start(bf16[32,2,384]{2,1,0:T(2,128)(2,1)} %reshape.55198), calls=%async_computation.1 | async-start | bytes 98304 | tf_op jit(solution)/shard_map/all_to_all | solution.py:158
  99.4 8.6 %all-to-all-done.1 = bf16[32,2,384]{2,1,0:T(2,128)(2,1)S(1)} async-done(((bf16[32,2,384]{2,1,0:T(2,128)(2,1)}), bf16[32,2,384]{2,1,0:T(2,128)(2,1)S(1)}, u32[]{:S(2)}, u32[]{:S(2)}) %all-to-all-start.1) | async-done | bytes 49184 | tf_op jit(solution)/shard_map/all_to_all | solution.py:158
  107.9 6.8 %all-to-all-start.3 = ((bf16[8,2,3072]{2,1,0:T(2,128)(2,1)}), bf16[8,2,3072]{2,1,0:T(2,128)(2,1)S(1)}, u32[]{:S(2)}, u32[]{:S(2)}) async-start(bf16[8,2,3072]{2,1,0:T(2,128)(2,1)} %reshape.55202), calls=%async_computation.3 | async-start | bytes 196608 | tf_op jit(solution)/shard_map/all_to_all | solution.py:204
  115.5 5.9 %fusion.2 = bf16[48,4,256]{2,0,1:T(8,128)(2,1)S(1)} fusion(bf16[48,4,128]{0,2,1:T(8,128)(2,1)S(1)} %bitcast.623, bf16[48,4,256]{2,0,1:T(8,128)(2,1)S(1)} %bitcast.596, f32[48,4]{0,1:T(4,128)S(1)} %bitcast.820, f32[48,4]{0,1:T(4,128)S(1)} %bitcast.821, f32[48,4]{0,1:T(4,128)S(1)} %bitcast.822, f32[48,4]{0,1:T(4,128)S(1)} %bitcast.823, ...), kind=kOutput, calls=%fused_computation.173 | convolution fusion | flops 25493504 | bytes 8339200 | tf_op jit(solution)/shard_map/dot_general | solution.py:217
  121.6 1.0 reshape.55200
  122.6 6.6 %all-to-all-start.2 = ((bf16[8,2,3072]{2,1,0:T(2,128)(2,1)}), bf16[8,2,3072]{2,1,0:T(2,128)(2,1)S(1)}, u32[]{:S(2)}, u32[]{:S(2)}) async-start(bf16[8,2,3072]{2,1,0:T(2,128)(2,1)} %reshape.55200), calls=%async_computation.2 | async-start | bytes 196608 | tf_op jit(solution)/shard_map/all_to_all | solution.py:240
  129.3 0.6 fusion.682
  130.6 6.3 %all-to-all-done.2 = bf16[8,2,3072]{2,1,0:T(2,128)(2,1)S(1)} async-done(((bf16[8,2,3072]{2,1,0:T(2,128)(2,1)}), bf16[8,2,3072]{2,1,0:T(2,128)(2,1)S(1)}, u32[]{:S(2)}, u32[]{:S(2)}) %all-to-all-start.2) | async-done | bytes 98336 | tf_op jit(solution)/shard_map/all_to_all | solution.py:240
  137.5 0.3 copy.376
  138.4 0.4 convolution_bitcast_fusion.1
  138.8 2.0 fusion.24
  140.9 0.3 fusion
  141.2 0.4 multiply_reduce_fusion
  142.0 1.0 reshape.55204
  143.0 3.4 all-to-all-start.4
  146.7 1.4 fusion.613
  148.1 5.7 %all-to-all-done.4 = bf16[8,2,3072]{2,1,0:T(2,128)(2,1)S(1)} async-done(((bf16[8,2,3072]{2,1,0:T(2,128)(2,1)}), bf16[8,2,3072]{2,1,0:T(2,128)(2,1)S(1)}, u32[]{:S(2)}, u32[]{:S(2)}) %all-to-all-start.4) | async-done | bytes 98336 | tf_op jit(solution)/shard_map/all_to_all | solution.py:249
  154.1 0.5 copy.433
  155.1 1.1 fusion.210
  156.2 1.2 fusion.219
  157.5 1.1 fusion.209
  158.6 1.2 fusion.218
  160.5 0.8 reshape.55206
  161.3 3.9 all-to-all-start.5
  165.2 3.0 collective-permute-start.2
  168.2 1.3 collective-permute-start.3
  169.5 0.8 fusion.217
  170.8 0.7 convolution_bitcast_fusion.6
  171.5 2.1 collective-permute-done.3
  174.2 0.3 convolution_bitcast_fusion.4
  175.2 0.8 reshape.55208
  176.0 10.8 %all-to-all-start.6 = ((bf16[32,2,384]{2,1,0:T(2,128)(2,1)}), bf16[32,2,384]{2,1,0:T(2,128)(2,1)S(1)}, u32[]{:S(2)}, u32[]{:S(2)}) async-start(bf16[32,2,384]{2,1,0:T(2,128)(2,1)} %reshape.55208), calls=%async_computation.6 | async-start | bytes 98304 | tf_op jit(solution)/shard_map/all_to_all | solution.py:158
  186.8 11.8 %all-reduce.5 = (f32[2,64,48]{1,2,0:T(8,128)S(1)}, f32[9,48]{1,0:T(8,128)S(1)}) all-reduce(f32[2,64,48]{1,2,0:T(8,128)S(1)} %pad_maximum_fusion.8, f32[9,48]{1,0:T(8,128)S(1)} %convolution_bitcast_fusion.6), channel_id=1, replica_groups=mesh['ens'=2,'lat'=32,'chan'=8] {'ens'}, use_global_device_ids=true, to_apply=%region_5.6 | all-reduce | flops 6576 | bytes 52608 | tf_op jit(solution)/shard_map/psum | solution.py:320
  198.6 115.7 %all-reduce.4 = (f32[2,64,48]{1,2,0:T(8,128)}, f32[9,48]{1,0:T(8,128)S(1)}) all-reduce(f32[2,64,48]{1,2,0:T(8,128)S(1)} %get-tuple-element.136, f32[9,48]{1,0:T(8,128)S(1)} %get-tuple-element.137), channel_id=1, replica_groups=mesh['ens'=2,'lat'=32,'chan'=8] {'lat'}, use_global_device_ids=true, to_apply=%region_6.7 | all-reduce | flops 6576 | bytes 52608 | tf_op jit(solution)/shard_map/psum | solution.py:320
  314.3 0.6 broadcast_multiply_fusion
  315.5 6.5 %fusion.4 = bf16[1,48,4,256]{3,1,2,0:T(8,128)(2,1)S(1)} fusion(bf16[48,4,128]{0,2,1:T(8,128)(2,1)S(1)} %bitcast.622, bf16[48,4,256]{2,0,1:T(8,128)(2,1)S(1)} %all_to_all.100, bf16[48,8,256]{2,0,1:T(8,128)(2,1)S(1)} %get-tuple-element.541, bf16[48,8,8]{2,0,1:T(8,128)(2,1)S(1)} %get-tuple-element.522, bf16[48,8,8]{2,0,1:T(8,128)(2,1)S(1)} %get-tuple-element.521, ...), kind=kOutput, calls=%fused_computation.177 | convolution fusion | flops 37191680 | bytes 1076992 | tf_op jit(solution)/shard_map/dot_general | solution.py:272
  322.1 0.7 copy.395
  322.8 110.1 %all-reduce.8.cloned.1.call-done = (f32[384,768]{1,0:T(8,128)}, f32[768,384]{1,0:T(8,128)}) async-done(((f32[384,768]{1,0:T(8,128)}, f32[768,384]{1,0:T(8,128)}), (f32[384,768]{1,0:T(8,128)}, f32[768,384]{1,0:T(8,128)})) %all-reduce.8.cloned.1.call-update) | async-done | bytes 2359312 | tf_op jit(solution)/shard_map/psum | solution.py:321
  432.9 1.5 dynamic-slice_multiply_fusion
  434.4 1.4 dynamic-slice_multiply_fusion.1
  (410 shorter events, 12.9 us)
Async XLA Ops:
  7.2 131.2 %copy-start = (bf16[384,768]{1,0:T(8,128)(2,1)S(1)}, bf16[384,768]{1,0:T(8,128)(2,1)}, u32[]{:S(2)}) copy-start(bf16[384,768]{1,0:T(8,128)(2,1)} %param.16) | copy-start | bytes 1769476
  8.4 63.4 %copy-start.5 = (s32[128,9]{0,1:T(8,128)S(1)}, s32[128,9]{0,1:T(8,128)}, u32[]{:S(2)}) copy-start(s32[128,9]{0,1:T(8,128)} %param.15) | copy-start | bytes 13828
  8.6 63.4 %copy-start.6 = (s32[128,9]{0,1:T(8,128)S(1)}, s32[128,9]{0,1:T(8,128)}, u32[]{:S(2)}) copy-start(s32[128,9]{0,1:T(8,128)} %param.14) | copy-start | bytes 13828
  8.6 63.7 %copy-start.3 = (f32[128,9]{0,1:T(8,128)S(1)}, f32[128,9]{0,1:T(8,128)}, u32[]{:S(2)}) copy-start(f32[128,9]{0,1:T(8,128)} %param.12) | copy-start | bytes 13828
  8.6 63.8 %copy-start.82 = (f32[9,48]{1,0:T(8,128)S(1)}, f32[9,48]{1,0:T(8,128)}, u32[]{:S(2)}) copy-start(f32[9,48]{1,0:T(8,128)} %param.13) | copy-start | bytes 5188
  9.7 76.3 %all-to-all-start = ((bf16[32,2,384]{2,1,0:T(2,128)(2,1)}), bf16[32,2,384]{2,1,0:T(2,128)(2,1)S(1)}, u32[]{:S(2)}, u32[]{:S(2)}) async-start(bf16[32,2,384]{2,1,0:T(2,128)(2,1)} %reshape.55196), calls=%async_computation | async-start | bytes 98304 | tf_op jit(solution)/shard_map/all_to_all | solution.py:154
  23.5 62.4 %collective-permute-start = (bf16[48,2,256]{2,0,1:T(8,128)(2,1)S(1)}, bf16[48,2,256]{2,0,1:T(8,128)(2,1)S(1)}, u32[]{:S(2)}, u32[]{:S(2)}) collective-permute-start(bf16[48,2,256]{2,0,1:T(8,128)(2,1)S(1)} %get-tuple-element.539), channel_id=1, source_target_pairs={{0,8},{8,16},{16,24},{24,32},{32,40},{40,48},{48,56},{56,64},{64,7... | collective-permute-start | bytes 147464 | tf_op jit(solution)/shard_map/ppermute | solution.py:20
  26.6 59.3 %collective-permute-start.1 = (bf16[48,2,256]{2,0,1:T(8,128)(2,1)S(1)}, bf16[48,2,256]{2,0,1:T(8,128)(2,1)S(1)}, u32[]{:S(2)}, u32[]{:S(2)}) collective-permute-start(bf16[48,2,256]{2,0,1:T(8,128)(2,1)S(1)} %get-tuple-element.538), channel_id=1, source_target_pairs={{8,0},{16,8},{24,16},{32,24},{40,32},{48,40},{56,48},{64,56},{72,6... | collective-permute-start | bytes 147464 | tf_op jit(solution)/shard_map/ppermute | solution.py:23
  87.8 27.3 %copy-start.36 = (f32[48,4,1,1]{0,3,2,1:T(1,128)S(1)}, f32[48,4,1,1]{0,3,2,1:T(1,128)}, u32[]{:S(2)}) copy-start(f32[48,4,1,1]{0,3,2,1:T(1,128)} %get-tuple-element.464) | copy-start | bytes 2308
  87.9 27.3 %copy-start.37 = (f32[48,4,1,1]{0,3,2,1:T(1,128)S(1)}, f32[48,4,1,1]{0,3,2,1:T(1,128)}, u32[]{:S(2)}) copy-start(f32[48,4,1,1]{0,3,2,1:T(1,128)} %get-tuple-element.465) | copy-start | bytes 2308
  87.9 27.3 %copy-start.38 = (f32[48,4,1,1]{0,3,2,1:T(1,128)S(1)}, f32[48,4,1,1]{0,3,2,1:T(1,128)}, u32[]{:S(2)}) copy-start(f32[48,4,1,1]{0,3,2,1:T(1,128)} %get-tuple-element.466) | copy-start | bytes 2308
  87.9 27.3 %copy-start.39 = (f32[48,4,1,1]{0,3,2,1:T(1,128)S(1)}, f32[48,4,1,1]{0,3,2,1:T(1,128)}, u32[]{:S(2)}) copy-start(f32[48,4,1,1]{0,3,2,1:T(1,128)} %get-tuple-element.467) | copy-start | bytes 2308
  87.9 27.3 %copy-start.40 = (f32[48,4,1,1]{0,3,2,1:T(1,128)S(1)}, f32[48,4,1,1]{0,3,2,1:T(1,128)}, u32[]{:S(2)}) copy-start(f32[48,4,1,1]{0,3,2,1:T(1,128)} %get-tuple-element.468) | copy-start | bytes 2308
  87.9 27.3 %copy-start.41 = (f32[48,4,1,1]{0,3,2,1:T(1,128)S(1)}, f32[48,4,1,1]{0,3,2,1:T(1,128)}, u32[]{:S(2)}) copy-start(f32[48,4,1,1]{0,3,2,1:T(1,128)} %get-tuple-element.469) | copy-start | bytes 2308
  87.9 27.3 %copy-start.42 = (f32[48,4,1,1]{0,3,2,1:T(1,128)S(1)}, f32[48,4,1,1]{0,3,2,1:T(1,128)}, u32[]{:S(2)}) copy-start(f32[48,4,1,1]{0,3,2,1:T(1,128)} %get-tuple-element.470) | copy-start | bytes 2308
  87.9 27.3 %copy-start.43 = (f32[48,4,1,1]{0,3,2,1:T(1,128)S(1)}, f32[48,4,1,1]{0,3,2,1:T(1,128)}, u32[]{:S(2)}) copy-start(f32[48,4,1,1]{0,3,2,1:T(1,128)} %get-tuple-element.471) | copy-start | bytes 2308
  87.9 27.3 %copy-start.44 = (f32[48,4,1,1]{0,3,2,1:T(1,128)S(1)}, f32[48,4,1,1]{0,3,2,1:T(1,128)}, u32[]{:S(2)}) copy-start(f32[48,4,1,1]{0,3,2,1:T(1,128)} %get-tuple-element.472) | copy-start | bytes 2308
  87.9 27.3 %copy-start.45 = (f32[48,4,1,1]{0,3,2,1:T(1,128)S(1)}, f32[48,4,1,1]{0,3,2,1:T(1,128)}, u32[]{:S(2)}) copy-start(f32[48,4,1,1]{0,3,2,1:T(1,128)} %get-tuple-element.473) | copy-start | bytes 2308
  87.9 27.3 %copy-start.46 = (f32[48,4,1,1]{0,3,2,1:T(1,128)S(1)}, f32[48,4,1,1]{0,3,2,1:T(1,128)}, u32[]{:S(2)}) copy-start(f32[48,4,1,1]{0,3,2,1:T(1,128)} %get-tuple-element.474) | copy-start | bytes 2308
  88.0 27.3 %copy-start.47 = (f32[48,4,1,1]{0,3,2,1:T(1,128)S(1)}, f32[48,4,1,1]{0,3,2,1:T(1,128)}, u32[]{:S(2)}) copy-start(f32[48,4,1,1]{0,3,2,1:T(1,128)} %get-tuple-element.475) | copy-start | bytes 2308
  88.0 27.3 %copy-start.48 = (f32[48,4,1,1]{0,3,2,1:T(1,128)S(1)}, f32[48,4,1,1]{0,3,2,1:T(1,128)}, u32[]{:S(2)}) copy-start(f32[48,4,1,1]{0,3,2,1:T(1,128)} %get-tuple-element.476) | copy-start | bytes 2308
  88.2 19.7 %all-to-all-start.1 = ((bf16[32,2,384]{2,1,0:T(2,128)(2,1)}), bf16[32,2,384]{2,1,0:T(2,128)(2,1)S(1)}, u32[]{:S(2)}, u32[]{:S(2)}) async-start(bf16[32,2,384]{2,1,0:T(2,128)(2,1)} %reshape.55198), calls=%async_computation.1 | async-start | bytes 98304 | tf_op jit(solution)/shard_map/all_to_all | solution.py:158
  107.9 14.7 %all-to-all-start.3 = ((bf16[8,2,3072]{2,1,0:T(2,128)(2,1)}), bf16[8,2,3072]{2,1,0:T(2,128)(2,1)S(1)}, u32[]{:S(2)}, u32[]{:S(2)}) async-start(bf16[8,2,3072]{2,1,0:T(2,128)(2,1)} %reshape.55202), calls=%async_computation.3 | async-start | bytes 196608 | tf_op jit(solution)/shard_map/all_to_all | solution.py:204
  122.6 14.2 %all-to-all-start.2 = ((bf16[8,2,3072]{2,1,0:T(2,128)(2,1)}), bf16[8,2,3072]{2,1,0:T(2,128)(2,1)S(1)}, u32[]{:S(2)}, u32[]{:S(2)}) async-start(bf16[8,2,3072]{2,1,0:T(2,128)(2,1)} %reshape.55200), calls=%async_computation.2 | async-start | bytes 196608 | tf_op jit(solution)/shard_map/all_to_all | solution.py:240
  143.0 10.9 %all-to-all-start.4 = ((bf16[8,2,3072]{2,1,0:T(2,128)(2,1)}), bf16[8,2,3072]{2,1,0:T(2,128)(2,1)S(1)}, u32[]{:S(2)}, u32[]{:S(2)}) async-start(bf16[8,2,3072]{2,1,0:T(2,128)(2,1)} %reshape.55204), calls=%async_computation.4 | async-start | bytes 196608 | tf_op jit(solution)/shard_map/all_to_all | solution.py:249
  146.4 286.5 %all-reduce.8.cloned.1.call-start = ((), (), s32[]{:S(2)}) async-start(), calls=%async_computation.7 | async-start | bytes 4718592 | tf_op jit(solution)/shard_map/psum | solution.py:321
  161.3 12.6 %all-to-all-start.5 = ((bf16[32,2,384]{2,1,0:T(2,128)(2,1)}), bf16[32,2,384]{2,1,0:T(2,128)(2,1)S(1)}, u32[]{:S(2)}, u32[]{:S(2)}) async-start(bf16[32,2,384]{2,1,0:T(2,128)(2,1)} %reshape.55206), calls=%async_computation.5 | async-start | bytes 98304 | tf_op jit(solution)/shard_map/all_to_all | solution.py:154
  165.2 6.3 %collective-permute-start.2 = (bf16[48,2,256]{2,0,1:T(8,128)(2,1)S(1)}, bf16[48,2,256]{2,0,1:T(8,128)(2,1)S(1)}, u32[]{:S(2)}, u32[]{:S(2)}) collective-permute-start(bf16[48,2,256]{2,0,1:T(8,128)(2,1)S(1)} %get-tuple-element.537), channel_id=1, source_target_pairs={{0,8},{8,16},{16,24},{24,32},{32,40},{40,48},{48,56},{56,64},{64,7... | collective-permute-start | bytes 147464 | tf_op jit(solution)/shard_map/ppermute | solution.py:20
  168.2 5.3 %collective-permute-start.3 = (bf16[48,2,256]{2,0,1:T(8,128)(2,1)S(1)}, bf16[48,2,256]{2,0,1:T(8,128)(2,1)S(1)}, u32[]{:S(2)}, u32[]{:S(2)}) collective-permute-start(bf16[48,2,256]{2,0,1:T(8,128)(2,1)S(1)} %get-tuple-element.536), channel_id=1, source_target_pairs={{8,0},{16,8},{24,16},{32,24},{40,32},{48,40},{56,48},{64,56},{72,6... | collective-permute-start | bytes 147464 | tf_op jit(solution)/shard_map/ppermute | solution.py:23
  174.5 140.8 %copy-start.7 = (f32[48,4,1,1]{0,3,2,1:T(1,128)S(1)}, f32[48,4,1,1]{0,3,2,1:T(1,128)}, u32[]{:S(2)}) copy-start(f32[48,4,1,1]{0,3,2,1:T(1,128)} %get-tuple-element.402) | copy-start | bytes 2308
  174.5 140.8 %copy-start.8 = (f32[48,4,1,1]{0,3,2,1:T(1,128)S(1)}, f32[48,4,1,1]{0,3,2,1:T(1,128)}, u32[]{:S(2)}) copy-start(f32[48,4,1,1]{0,3,2,1:T(1,128)} %get-tuple-element.403) | copy-start | bytes 2308
  174.5 140.8 %copy-start.9 = (f32[48,4,1,1]{0,3,2,1:T(1,128)S(1)}, f32[48,4,1,1]{0,3,2,1:T(1,128)}, u32[]{:S(2)}) copy-start(f32[48,4,1,1]{0,3,2,1:T(1,128)} %get-tuple-element.404) | copy-start | bytes 2308
  174.5 140.8 %copy-start.10 = (f32[48,4,1,1]{0,3,2,1:T(1,128)S(1)}, f32[48,4,1,1]{0,3,2,1:T(1,128)}, u32[]{:S(2)}) copy-start(f32[48,4,1,1]{0,3,2,1:T(1,128)} %get-tuple-element.405) | copy-start | bytes 2308
  174.5 140.8 %copy-start.11 = (f32[48,4,1,1]{0,3,2,1:T(1,128)S(1)}, f32[48,4,1,1]{0,3,2,1:T(1,128)}, u32[]{:S(2)}) copy-start(f32[48,4,1,1]{0,3,2,1:T(1,128)} %get-tuple-element.406) | copy-start | bytes 2308
  174.5 140.8 %copy-start.12 = (f32[48,4,1,1]{0,3,2,1:T(1,128)S(1)}, f32[48,4,1,1]{0,3,2,1:T(1,128)}, u32[]{:S(2)}) copy-start(f32[48,4,1,1]{0,3,2,1:T(1,128)} %get-tuple-element.407) | copy-start | bytes 2308
  174.5 140.8 %copy-start.13 = (f32[48,4,1,1]{0,3,2,1:T(1,128)S(1)}, f32[48,4,1,1]{0,3,2,1:T(1,128)}, u32[]{:S(2)}) copy-start(f32[48,4,1,1]{0,3,2,1:T(1,128)} %get-tuple-element.408) | copy-start | bytes 2308
  174.5 140.8 %copy-start.14 = (f32[48,4,1,1]{0,3,2,1:T(1,128)S(1)}, f32[48,4,1,1]{0,3,2,1:T(1,128)}, u32[]{:S(2)}) copy-start(f32[48,4,1,1]{0,3,2,1:T(1,128)} %get-tuple-element.409) | copy-start | bytes 2308
  174.5 140.8 %copy-start.15 = (f32[48,4,1,1]{0,3,2,1:T(1,128)S(1)}, f32[48,4,1,1]{0,3,2,1:T(1,128)}, u32[]{:S(2)}) copy-start(f32[48,4,1,1]{0,3,2,1:T(1,128)} %get-tuple-element.410) | copy-start | bytes 2308
  174.5 140.8 %copy-start.16 = (f32[48,4,1,1]{0,3,2,1:T(1,128)S(1)}, f32[48,4,1,1]{0,3,2,1:T(1,128)}, u32[]{:S(2)}) copy-start(f32[48,4,1,1]{0,3,2,1:T(1,128)} %get-tuple-element.411) | copy-start | bytes 2308
  174.6 140.8 %copy-start.17 = (f32[48,4,1,1]{0,3,2,1:T(1,128)S(1)}, f32[48,4,1,1]{0,3,2,1:T(1,128)}, u32[]{:S(2)}) copy-start(f32[48,4,1,1]{0,3,2,1:T(1,128)} %get-tuple-element.412) | copy-start | bytes 2308
  174.6 140.8 %copy-start.18 = (f32[48,4,1,1]{0,3,2,1:T(1,128)S(1)}, f32[48,4,1,1]{0,3,2,1:T(1,128)}, u32[]{:S(2)}) copy-start(f32[48,4,1,1]{0,3,2,1:T(1,128)} %get-tuple-element.413) | copy-start | bytes 2308
  174.6 140.8 %copy-start.19 = (f32[48,4,1,1]{0,3,2,1:T(1,128)S(1)}, f32[48,4,1,1]{0,3,2,1:T(1,128)}, u32[]{:S(2)}) copy-start(f32[48,4,1,1]{0,3,2,1:T(1,128)} %get-tuple-element.414) | copy-start | bytes 2308
  174.6 140.8 %copy-start.20 = (f32[48,4,1,1]{0,3,2,1:T(1,128)S(1)}, f32[48,4,1,1]{0,3,2,1:T(1,128)}, u32[]{:S(2)}) copy-start(f32[48,4,1,1]{0,3,2,1:T(1,128)} %get-tuple-element.415) | copy-start | bytes 2308
  174.6 140.8 %copy-start.21 = (f32[48,4,1,1]{0,3,2,1:T(1,128)S(1)}, f32[48,4,1,1]{0,3,2,1:T(1,128)}, u32[]{:S(2)}) copy-start(f32[48,4,1,1]{0,3,2,1:T(1,128)} %get-tuple-element.416) | copy-start | bytes 2308
  174.6 140.8 %copy-start.22 = (f32[48,4,1,1]{0,3,2,1:T(1,128)S(1)}, f32[48,4,1,1]{0,3,2,1:T(1,128)}, u32[]{:S(2)}) copy-start(f32[48,4,1,1]{0,3,2,1:T(1,128)} %get-tuple-element.417) | copy-start | bytes 2308
  174.6 140.8 %copy-start.23 = (f32[48,4,1,1]{0,3,2,1:T(1,128)S(1)}, f32[48,4,1,1]{0,3,2,1:T(1,128)}, u32[]{:S(2)}) copy-start(f32[48,4,1,1]{0,3,2,1:T(1,128)} %get-tuple-element.418) | copy-start | bytes 2308
  174.6 140.8 %copy-start.24 = (f32[48,4,1,1]{0,3,2,1:T(1,128)S(1)}, f32[48,4,1,1]{0,3,2,1:T(1,128)}, u32[]{:S(2)}) copy-start(f32[48,4,1,1]{0,3,2,1:T(1,128)} %get-tuple-element.419) | copy-start | bytes 2308
  174.6 140.8 %copy-start.25 = (f32[48,4,1,1]{0,3,2,1:T(1,128)S(1)}, f32[48,4,1,1]{0,3,2,1:T(1,128)}, u32[]{:S(2)}) copy-start(f32[48,4,1,1]{0,3,2,1:T(1,128)} %get-tuple-element.420) | copy-start | bytes 2308
  174.6 140.8 %copy-start.26 = (f32[48,4,1,1]{0,3,2,1:T(1,128)S(1)}, f32[48,4,1,1]{0,3,2,1:T(1,128)}, u32[]{:S(2)}) copy-start(f32[48,4,1,1]{0,3,2,1:T(1,128)} %get-tuple-element.421) | copy-start | bytes 2308
  174.7 140.8 %copy-start.27 = (f32[48,4,1,1]{0,3,2,1:T(1,128)S(1)}, f32[48,4,1,1]{0,3,2,1:T(1,128)}, u32[]{:S(2)}) copy-start(f32[48,4,1,1]{0,3,2,1:T(1,128)} %get-tuple-element.422) | copy-start | bytes 2308
  174.7 140.8 %copy-start.28 = (f32[48,4,1,1]{0,3,2,1:T(1,128)S(1)}, f32[48,4,1,1]{0,3,2,1:T(1,128)}, u32[]{:S(2)}) copy-start(f32[48,4,1,1]{0,3,2,1:T(1,128)} %get-tuple-element.423) | copy-start | bytes 2308
  174.7 140.8 %copy-start.29 = (f32[48,4,1,1]{0,3,2,1:T(1,128)S(1)}, f32[48,4,1,1]{0,3,2,1:T(1,128)}, u32[]{:S(2)}) copy-start(f32[48,4,1,1]{0,3,2,1:T(1,128)} %get-tuple-element.424) | copy-start | bytes 2308
  174.7 140.8 %copy-start.30 = (f32[48,4,1,1]{0,3,2,1:T(1,128)S(1)}, f32[48,4,1,1]{0,3,2,1:T(1,128)}, u32[]{:S(2)}) copy-start(f32[48,4,1,1]{0,3,2,1:T(1,128)} %get-tuple-element.425) | copy-start | bytes 2308
  174.7 140.8 %copy-start.31 = (f32[48,4,1,1]{0,3,2,1:T(1,128)S(1)}, f32[48,4,1,1]{0,3,2,1:T(1,128)}, u32[]{:S(2)}) copy-start(f32[48,4,1,1]{0,3,2,1:T(1,128)} %get-tuple-element.426) | copy-start | bytes 2308
  174.7 140.8 %copy-start.72 = (f32[48,4,1,1]{0,3,2,1:T(1,128)S(1)}, f32[48,4,1,1]{0,3,2,1:T(1,128)}, u32[]{:S(2)}) copy-start(f32[48,4,1,1]{0,3,2,1:T(1,128)} %get-tuple-element.427) | copy-start | bytes 2308
  174.7 140.8 %copy-start.73 = (f32[48,4,1,1]{0,3,2,1:T(1,128)S(1)}, f32[48,4,1,1]{0,3,2,1:T(1,128)}, u32[]{:S(2)}) copy-start(f32[48,4,1,1]{0,3,2,1:T(1,128)} %get-tuple-element.428) | copy-start | bytes 2308
  174.7 140.8 %copy-start.74 = (f32[48,4,1,1]{0,3,2,1:T(1,128)S(1)}, f32[48,4,1,1]{0,3,2,1:T(1,128)}, u32[]{:S(2)}) copy-start(f32[48,4,1,1]{0,3,2,1:T(1,128)} %get-tuple-element.429) | copy-start | bytes 2308
  174.7 140.8 %copy-start.75 = (f32[48,4,1,1]{0,3,2,1:T(1,128)S(1)}, f32[48,4,1,1]{0,3,2,1:T(1,128)}, u32[]{:S(2)}) copy-start(f32[48,4,1,1]{0,3,2,1:T(1,128)} %get-tuple-element.430) | copy-start | bytes 2308
  174.7 140.8 %copy-start.76 = (f32[48,4,1,1]{0,3,2,1:T(1,128)S(1)}, f32[48,4,1,1]{0,3,2,1:T(1,128)}, u32[]{:S(2)}) copy-start(f32[48,4,1,1]{0,3,2,1:T(1,128)} %get-tuple-element.431) | copy-start | bytes 2308
  174.8 140.8 %copy-start.77 = (f32[48,4,1,1]{0,3,2,1:T(1,128)S(1)}, f32[48,4,1,1]{0,3,2,1:T(1,128)}, u32[]{:S(2)}) copy-start(f32[48,4,1,1]{0,3,2,1:T(1,128)} %get-tuple-element.432) | copy-start | bytes 2308
  174.8 140.8 %copy-start.78 = (f32[48,4,1,1]{0,3,2,1:T(1,128)S(1)}, f32[48,4,1,1]{0,3,2,1:T(1,128)}, u32[]{:S(2)}) copy-start(f32[48,4,1,1]{0,3,2,1:T(1,128)} %get-tuple-element.433) | copy-start | bytes 2308
  174.8 140.8 %copy-start.79 = (f32[48,4,1,1]{0,3,2,1:T(1,128)S(1)}, f32[48,4,1,1]{0,3,2,1:T(1,128)}, u32[]{:S(2)}) copy-start(f32[48,4,1,1]{0,3,2,1:T(1,128)} %get-tuple-element.434) | copy-start | bytes 2308
  174.8 140.8 %copy-start.80 = (f32[48,4,1,1]{0,3,2,1:T(1,128)S(1)}, f32[48,4,1,1]{0,3,2,1:T(1,128)}, u32[]{:S(2)}) copy-start(f32[48,4,1,1]{0,3,2,1:T(1,128)} %get-tuple-element.435) | copy-start | bytes 2308
  176.0 138.8 %all-to-all-start.6 = ((bf16[32,2,384]{2,1,0:T(2,128)(2,1)}), bf16[32,2,384]{2,1,0:T(2,128)(2,1)S(1)}, u32[]{:S(2)}, u32[]{:S(2)}) async-start(bf16[32,2,384]{2,1,0:T(2,128)(2,1)} %reshape.55208), calls=%async_computation.6 | async-start | bytes 98304 | tf_op jit(solution)/shard_map/all_to_all | solution.py:158
  (31 other events, 743.9 us)
Sparse Core Ops, SparseCore 0:
  152.3 280.4 all-reduce.7
